TPU v7x, 512 devices: a whole 4x4x16 slice. The times are simulated.
512 devices in a mesh: visit: 8 (over y, core), sky: 64 (over x, z).
Axes of the slice: x: 4, y: 4, z: 16, core: 2. Of those that a mesh axis runs over, the one named last changes fastest.
Arguments:
- raw_tiles: float32 [28672, 128, 128], P(('visit', 'sky')), may hold values from -4 to 4
- warp_shift: int32 [28672, 2], P(('visit', 'sky')), may hold values from -2 to 2
- warp_taps: float32 [28672, 2, 4], P(('visit', 'sky')), may hold values from -0.25 to 1
- match_coeffs: float32 [28672, 27], P(('visit', 'sky')), may hold values from -3 to 3
- tile_weights: float32 [28672], P(('visit', 'sky')), may hold values from 0.5 to 2
- dest_owner: int32 [28672, 1], P(('visit', 'sky')), may hold values from 0 to 63; in each aligned block of 56 rows (0 to 55, 56 to 111, ...) at most 2 rows name the same one
- dest_cell: int32 [28672], P(('visit', 'sky')), may hold values from 0 to 15
- template: float32 [16384, 1024], P('sky'), may hold values from -6 to 6
- basis_rows: float32 [9, 31], replicated, may hold values from -1 to 1
- basis_cols: float32 [9, 31], replicated, may hold values from -1 to 1
Outputs:
- coadd: float32 [16384, 1024], P('sky', 'visit')
Inputs may be any that keep to these rules, and one draw needn't show every extreme that they name: `dest_owner`: among the tiles of one device no owner is named more than 2 times, a bound that some block reaches.
All inputs are finite; a program needn't handle non-finite values.
Results may differ from a plain program's by a relative error of at most 0.0003.
Values sent between devices are 32-bit elements; how exact they have to be, the bound alone decides.
A program may use at most 128 MiB of HBM per device.

v0:
```python
import jax
import jax.numpy as jnp
from jax import lax
from jax.sharding import PartitionSpec as P


def extended(x, sides, width):
    for axis, dim in sides:
        devices, length = (lax.axis_size(axis), x.shape[dim])
        up = [(i, (i + 1) % devices) for i in range(devices - 1)]
        down = [(j, i) for i, j in up]
        last = lax.slice_in_dim(x, length - width, length, axis=dim)
        initial = lax.slice_in_dim(x, 0, width, axis=dim)
        before = lax.ppermute(last, axis, up)
        after = lax.ppermute(initial, axis, down)
        x = jnp.concatenate([before, x, after], axis=dim)
    return x


def warp_matrix(shift, taps, size):
    idx = jnp.arange(size, dtype=jnp.int32)
    offset = idx[None, None, :] - idx[None, :, None] - shift[:, None, None] + 1
    total = jnp.zeros(offset.shape, jnp.float32)
    for tap in range(taps.shape[1]):
        total = total + jnp.where(offset == tap, taps[:, tap][:, None, None], jnp.float32(0.0))
    return total


def band_matrix(kernel, outer, inner):
    ksize = kernel.shape[1]
    offset = jnp.arange(outer)[:, None] - jnp.arange(inner)[None, :]
    picks = (offset[:, :, None] == jnp.arange(ksize)[None, None, :]).astype(jnp.float32)
    return jnp.einsum("bt,kjt->bkj", kernel, picks, precision=lax.Precision.HIGHEST)


def model_block(textpad, coef_cells, basis_rows, basis_cols, start, width, tile):
    ksize = basis_rows.shape[1]
    rows_n = textpad.shape[0] - ksize + 1
    cols_n = textpad.shape[1] - ksize + 1
    nb = basis_rows.shape[0]
    block = lax.dynamic_slice_in_dim(textpad, start, width + ksize - 1, 1)
    across = band_matrix(basis_cols, width + ksize - 1, width)
    down = band_matrix(basis_rows, rows_n + ksize - 1, rows_n)
    middle = jnp.einsum("rk,bkj->brj", block, across, precision=lax.Precision.HIGHEST)
    conv = jnp.einsum("bki,bkj->bij", down, middle, precision=lax.Precision.HIGHEST)
    cell_rows = rows_n // tile
    cell_cols = cols_n // tile
    table = coef_cells.reshape(cell_rows, cell_cols, nb, 3)
    columns = start + jnp.arange(width)
    select = (columns[:, None] // tile == jnp.arange(cell_cols)[None, :]).astype(jnp.float32)
    percol = jnp.einsum("wc,rcbk->rwbk", select, table, precision=lax.Precision.HIGHEST)
    xcoord = (2.0 * (columns % tile).astype(jnp.float32) + 1.0) / tile - 1.0
    ycoord = (2.0 * jnp.arange(tile).astype(jnp.float32) + 1.0) / tile - 1.0
    conv4 = conv.reshape(nb, cell_rows, tile, width)
    flat = percol[..., 0] + percol[..., 1] * xcoord[None, :, None]
    slope = percol[..., 2]
    model = jnp.einsum("briw,rwb->riw", conv4, flat, precision=lax.Precision.HIGHEST)
    model = model + ycoord[None, :, None] * jnp.einsum(
        "briw,rwb->riw", conv4, slope, precision=lax.Precision.HIGHEST
    )
    return model.reshape(rows_n, width)


def pack_slots(owner, rank, lowest, slots, sky_n, weighted, meta):
    chosen = jnp.logical_and(rank >= lowest, rank < lowest + slots)
    slot = owner * slots + rank - lowest
    placing = jnp.logical_and(
        jnp.arange(sky_n * slots)[:, None] == slot[None, :], chosen[None, :]
    ).astype(jnp.float32)
    outgoing = jnp.dot(placing, weighted, precision=lax.Precision.HIGHEST).reshape(
        sky_n, slots, weighted.shape[1]
    )
    out_meta = jnp.dot(placing, meta, precision=lax.Precision.HIGHEST).reshape(
        sky_n, slots, meta.shape[1]
    )
    return (outgoing, out_meta)


def place_cells(incoming, in_meta, cells):
    incoming = incoming.reshape(-1, incoming.shape[2])
    in_meta = in_meta.reshape(-1, in_meta.shape[2])
    cell_of = in_meta[:, -1]
    gather_cells = (jnp.arange(cells).astype(jnp.float32)[:, None] == cell_of[None, :]).astype(
        jnp.float32
    )
    sci_cells = jnp.dot(gather_cells, incoming, precision=lax.Precision.HIGHEST)
    coef_cells = jnp.dot(gather_cells, in_meta[:, :-1], precision=lax.Precision.HIGHEST)
    return (sci_cells, coef_cells)


def body(
    raw_tiles,
    warp_shift,
    warp_taps,
    match_coeffs,
    tile_weights,
    dest_owner,
    dest_cell,
    template,
    basis_rows,
    basis_cols,
):
    tile = raw_tiles.shape[1]
    count = raw_tiles.shape[0]
    sky_n = lax.axis_size("sky")
    visit_n = lax.axis_size("visit")
    capacity = max(2, (2 * count + sky_n - 1) // sky_n)
    rows_n, cols_n = template.shape
    cells = rows_n // tile * (cols_n // tile)
    half = basis_rows.shape[1] // 2
    m_rows = warp_matrix(warp_shift[:, 0], warp_taps[:, 0, :], tile)
    m_cols = warp_matrix(warp_shift[:, 1], warp_taps[:, 1, :], tile)
    warped = jnp.einsum("tik,tkl->til", m_rows, raw_tiles, precision=lax.Precision.HIGHEST)
    warped = jnp.einsum("til,tjl->tij", warped, m_cols, precision=lax.Precision.HIGHEST)
    weighted = (warped * tile_weights[:, None, None]).reshape(count, tile * tile)
    meta = jnp.concatenate(
        [match_coeffs * tile_weights[:, None], dest_cell.astype(jnp.float32)[:, None]], axis=1
    )
    owner = dest_owner[:, 0]
    same = owner[:, None] == owner[None, :]
    earlier = jnp.arange(count)[None, :] < jnp.arange(count)[:, None]
    rank = jnp.sum(jnp.logical_and(same, earlier).astype(jnp.int32), axis=1)
    textpad = extended(template, (("sky", 0),), half)
    textpad = jnp.pad(textpad, ((0, 0), (half, half)))
    outgoing, out_meta = pack_slots(owner, rank, 0, capacity, sky_n, weighted, meta)
    incoming, in_meta = (
        lax.all_to_all(outgoing, "sky", split_axis=0, concat_axis=0, tiled=True),
        lax.all_to_all(out_meta, "sky", split_axis=0, concat_axis=0, tiled=True),
    )
    sci_cells, coef_cells = place_cells(incoming, in_meta, cells)
    sci_img = (
        sci_cells.reshape(rows_n // tile, cols_n // tile, tile, tile)
        .transpose(0, 2, 1, 3)
        .reshape(rows_n, cols_n)
    )
    width = cols_n // visit_n
    pieces = []
    for part in range(visit_n):
        pieces.append(
            model_block(textpad, coef_cells, basis_rows, basis_cols, part * width, width, tile)
        )
    model = jnp.concatenate(pieces, axis=1)
    return lax.psum_scatter(sci_img - model, "visit", scatter_dimension=1, tiled=True)


def solution(mesh):
    return jax.shard_map(
        body,
        mesh=mesh,
        in_specs=(
            P(("visit", "sky"), None, None),
            P(("visit", "sky"), None),
            P(("visit", "sky"), None, None),
            P(("visit", "sky"), None),
            P(("visit", "sky")),
            P(("visit", "sky"), None),
            P(("visit", "sky")),
            P("sky", None),
            P(),
            P(),
        ),
        out_specs=P("sky", "visit"),
        check_vma=False,
    )
```

profile of v0, /device:TPU:1, one launch (start us, length us, event | category | flops | bytes accessed | tf_op | source)
XLA Modules:
  0.0 590.9 jit_solution(1362774169525247955)
XLA Ops:
  6.5 0.9 convert_reduce_fusion
  7.5 0.7 multiply_add_fusion.10
  8.1 0.7 convert_bitcast_fusion
  8.8 0.7 broadcast_multiply_fusion
  9.5 0.8 fusion.78
  10.3 19.1 %all-to-all-start = ((f32[64,2,28]{2,1,0:T(2,128)}), f32[64,2,28]{2,1,0:T(2,128)S(1)}, u32[]{:S(2)}, u32[]{:S(2)}) async-start(f32[64,2,28]{2,1,0:T(2,128)} %bitcast.18), calls=%async_computation | async-start | bytes 131072 | tf_op jit(solution)/shard_map/all_to_all | solution.py:128
  29.5 0.7 slice_bitcast_fusion.36
  30.2 0.8 slice_bitcast_fusion.42
  30.9 7.5 %fusion.14 = f32[56,128,128]{2,1,0:T(8,128)S(1)} fusion(f32[56,128,128]{2,1,0:T(8,128)} %param.10, f32[56]{0:T(128)S(1)} %get-tuple-element.53, f32[56]{0:T(128)S(1)} %get-tuple-element.52, f32[56]{0:T(128)S(1)} %get-tuple-element.51, f32[56]{0:T(128)S(1)} %get-tuple-element.54, s32[56]{0:T(128)S(1)} %get-tuple-element.34, ...), kind=kOutput, calls=%fused_computation.16 | convolution fusion | flops 1421213696 | bytes 7406688 | tf_op jit(solution)/shard_map/tik,tkl->til/dot_general | solution.py:113
  38.4 10.8 %fusion.36 = f32[56,128,128]{2,1,0:T(8,128)} fusion(f32[56,128,128]{2,1,0:T(8,128)S(1)} %fusion.14, f32[56]{0:T(128)S(1)} %copy-done.5, f32[56]{0:T(128)S(1)} %get-tuple-element.26, f32[56]{0:T(128)S(1)} %get-tuple-element.27, f32[56]{0:T(128)S(1)} %get-tuple-element.28, f32[56]{0:T(128)S(1)} %get-tuple-element.25, s32[56]{0:T(128)S(1)} %get-tuple-element.33, ...), kind=kOutput, calls=%fused_computation.32 | convolution fusion | flops 1422131200 | bytes 7406912 | tf_op jit(solution)/shard_map/til,tjl->tij/dot_general | solution.py:114
  49.2 4.8 reshape.665
  54.0 5.7 fusion.80
  59.8 7.9 %copy.142 = f32[64,2,16384]{2,1,0:T(2,128)} copy(f32[64,2,16384]{2,0,1:T(8,128)S(1)} %fusion.80) | data formatting | bytes 16777216 | tf_op jit(solution)/shard_map/dot_general | solution.py:70
  67.6 15.0 %all-to-all-start.1 = ((f32[64,2,16384]{2,1,0:T(2,128)}), f32[64,2,16384]{2,1,0:T(2,128)}, u32[]{:S(2)}, u32[]{:S(2)}) async-start(f32[64,2,16384]{2,1,0:T(2,128)} %copy.142), calls=%async_computation.1 | async-start | bytes 16777216 | tf_op jit(solution)/shard_map/all_to_all | solution.py:127
  82.7 1.0 copy.147
  83.7 3.7 collective-permute-start
  87.4 1.0 copy.148
  88.4 1.7 collective-permute-start.1
  90.1 1.3 copy.149
  91.5 1.0 fusion.61
  92.8 4.0 fusion.35
  96.8 1.5 copy.151
  101.5 350.4 %collective-permute-done = f32[15,1024]{0,1:T(8,128)} collective-permute-done((f32[15,1024]{0,1:T(8,128)}, f32[15,1024]{0,1:T(8,128)}, u32[]{:S(2)}, u32[]{:S(2)}) %collective-permute-start) | collective-permute-done | bytes 61472 | tf_op jit(solution)/shard_map/ppermute | solution.py:14
  451.9 2.5 collective-permute-done.1
  454.4 1.8 pad_maximum_fusion
  456.2 1.4 fusion.70
  457.6 1.4 fusion.71
  459.0 6.0 %fusion.201 = f32[9,256,128]{2,1,0:T(8,128)S(1)} fusion(f32[9,286,256]{2,1,0:T(8,128)S(1)} %copy.151, f32[9,128,286]{1,2,0:T(8,128)S(1)} %fusion.70), kind=kOutput, calls=%fused_computation.340 | convolution fusion | flops 1012137984 | bytes 5133312 | tf_op jit(solution)/shard_map/bki,bkj->bij/dot_general | solution.py:45
  465.0 5.9 fusion.200
  470.9 0.4 multiply_reduce_fusion.4
  471.3 1.6 fusion.73
  472.9 1.4 fusion.72
  474.3 5.9 fusion.198
  480.2 6.3 %fusion.199 = f32[9,256,128]{2,1,0:T(8,128)S(1)} fusion(f32[9,286,256]{2,1,0:T(8,128)S(1)} %copy.151, f32[9,128,286]{1,2,0:T(8,128)S(1)} %fusion.72), kind=kOutput, calls=%fused_computation.338 | convolution fusion | flops 1012137984 | bytes 5133312 | tf_op jit(solution)/shard_map/bki,bkj->bij/dot_general | solution.py:45
  486.9 1.4 fusion.64
  488.2 1.4 fusion.74
  489.6 5.9 fusion.196
  495.5 6.0 %fusion.197 = f32[9,256,128]{2,1,0:T(8,128)S(1)} fusion(f32[9,286,256]{2,1,0:T(8,128)S(1)} %copy.151, f32[9,128,286]{1,2,0:T(8,128)S(1)} %fusion.74), kind=kOutput, calls=%fused_computation.336 | convolution fusion | flops 1012137984 | bytes 5133312 | tf_op jit(solution)/shard_map/bki,bkj->bij/dot_general | solution.py:45
  501.5 0.4 multiply_reduce_fusion.12
  502.0 1.4 fusion.67
  503.4 1.4 fusion.69
  504.7 6.1 %fusion.202 = f32[9,256,128]{2,1,0:T(8,128)S(1)} fusion(f32[9,286,256]{2,1,0:T(8,128)S(1)} %copy.151, f32[9,128,286]{1,2,0:T(8,128)S(1)} %fusion.69), kind=kOutput, calls=%fused_computation.341 | convolution fusion | flops 1012137984 | bytes 5133312 | tf_op jit(solution)/shard_map/bki,bkj->bij/dot_general | solution.py:45
  510.8 5.9 fusion.203
  517.5 10.9 %reshape.646 = f32[128,16384]{1,0:T(8,128)} reshape(f32[64,2,16384]{2,1,0:T(2,128)} %all-to-all-done.1) | data formatting | bytes 16777216 | tf_op jit(solution)/shard_map/reshape | solution.py:80
  528.3 9.0 %copy.143 = f32[16384,128]{1,0:T(8,128)} copy(f32[16384,128]{0,1:T(8,128)} %bitcast.349) | data formatting | bytes 16777216 | tf_op jit(solution)/shard_map/dot_general | solution.py:86
  537.3 6.3 %fusion.110 = f32[2,8,128,128]{3,1,2,0:T(8,128)S(1)} fusion(f32[128,128,128,1]{2,1,0,3:T(8,128)} %bitcast.348, f32[128]{0:T(128)S(1)} %slice_reduce_fusion, f32[2,8]{1,0:T(2,128)S(1)} %add_convert_fusion), kind=kOutput, calls=%fused_computation.183 | convolution fusion | flops 402655232 | bytes 9437760 | tf_op jit(solution)/shard_map/dot_general | solution.py:86
  543.7 1.3 bitcast_subtract_fusion
  545.0 38.7 %reduce-scatter.2.cloned.1.call-done = f32[256,128]{1,0:T(8,128)} async-done(((f32[256,1024]{1,0:T(8,128)}), f32[256,128]{1,0:T(8,128)}) %reduce-scatter.2.cloned.1.call-update) | async-done | bytes 131088 | tf_op jit(solution)/shard_map/reduce_scatter | solution.py:143
  (98 shorter events, 4.2 us)
Async XLA Ops:
  6.5 86.3 %copy-start = (f32[9,31]{1,0:T(8,128)S(1)}, f32[9,31]{1,0:T(8,128)}, u32[]{:S(2)}) copy-start(f32[9,31]{1,0:T(8,128)} %param.18) | copy-start | bytes 3352
  10.3 57.3 %all-to-all-start = ((f32[64,2,28]{2,1,0:T(2,128)}), f32[64,2,28]{2,1,0:T(2,128)S(1)}, u32[]{:S(2)}, u32[]{:S(2)}) async-start(f32[64,2,28]{2,1,0:T(2,128)} %bitcast.18), calls=%async_computation | async-start | bytes 131072 | tf_op jit(solution)/shard_map/all_to_all | solution.py:128
  30.9 7.5 %copy-start.5 = (f32[56]{0:T(128)S(1)}, f32[56]{0:T(128)}, u32[]{:S(2)}) copy-start(f32[56]{0:T(128)} %param.14) | copy-start | bytes 676
  67.6 15.0 %copy-start.3 = (f32[256,1024]{1,0:T(8,128)S(1)}, f32[256,1024]{1,0:T(8,128)}, u32[]{:S(2)}) copy-start(f32[256,1024]{1,0:T(8,128)} %param.17) | copy-start | bytes 3145732
  67.6 449.8 %all-to-all-start.1 = ((f32[64,2,16384]{2,1,0:T(2,128)}), f32[64,2,16384]{2,1,0:T(2,128)}, u32[]{:S(2)}, u32[]{:S(2)}) async-start(f32[64,2,16384]{2,1,0:T(2,128)} %copy.142), calls=%async_computation.1 | async-start | bytes 16777216 | tf_op jit(solution)/shard_map/all_to_all | solution.py:127
  82.6 501.1 %reduce-scatter.2.cloned.1.call-start = ((), (), s32[]{:S(2)}) async-start(), calls=%async_computation.3 | async-start | bytes 1179648 | tf_op jit(solution)/shard_map/reduce_scatter | solution.py:143
  82.7 8.8 %copy-start.4 = (f32[9,31]{1,0:T(8,128)S(1)}, f32[9,31]{1,0:T(8,128)}, u32[]{:S(2)}) copy-start(f32[9,31]{1,0:T(8,128)} %param.19) | copy-start | bytes 3352
  83.7 368.2 %collective-permute-start = (f32[15,1024]{0,1:T(8,128)}, f32[15,1024]{0,1:T(8,128)}, u32[]{:S(2)}, u32[]{:S(2)}) collective-permute-start(f32[15,1024]{0,1:T(8,128)} %copy.147), channel_id=1, source_target_pairs={{0,1},{1,2},{2,3},{3,4},{4,5},{5,6},{6,7},{7,8},{8,9},{9,10},{10,1... | collective-permute-start | bytes 184328 | tf_op jit(solution)/shard_map/ppermute | solution.py:14
  88.4 365.9 %collective-permute-start.1 = (f32[15,1024]{0,1:T(8,128)}, f32[15,1024]{0,1:T(8,128)}, u32[]{:S(2)}, u32[]{:S(2)}) collective-permute-start(f32[15,1024]{0,1:T(8,128)} %copy.148), channel_id=1, source_target_pairs={{1,0},{2,1},{3,2},{4,3},{5,4},{6,5},{7,6},{8,7},{9,8},{10,9},{11,1... | collective-permute-start | bytes 184328 | tf_op jit(solution)/shard_map/ppermute | solution.py:15
  99.2 355.2 %copy-start.2 = (f32[256,1024]{0,1:T(8,128)S(1)}, f32[256,1024]{0,1:T(8,128)}, u32[]{:S(2)}) copy-start(f32[256,1024]{0,1:T(8,128)} %copy.149) | copy-start | bytes 3145732
  543.6 40.1 %copy-start.1 = (f32[9,31]{1,0:T(8,128)S(1)}, f32[9,31]{1,0:T(8,128)}, u32[]{:S(2)}) copy-start(f32[9,31]{1,0:T(8,128)} %param.18) | copy-start | bytes 3352
Sparse Core Ops, SparseCore 0:
  545.1 38.5 reduce-scatter.1
where the time goes:
time: 602 us; the launch traced here: 591 us
  waiting for transfers between devices  392 us (65%)
  matrix products  97.3 us (16%)
  local copies, waits for them, and re-layouts  39.8 us (7%)
  starting transfers between devices  39.5 us (7%)
  between operations  14.6 us (2%)
  other arithmetic  8.17 us (1%)
    ppermute x1, waiting for transfers between devices, extended(): before = lax.ppermute(last, axis, up)  350 us
    dot_general x8, matrix products, model_block(): jnp.einsum('bki,bkj->bij', down, middle, precision=lax.Precision.HIGHEST)  47.9 us
    reduce_scatter x1, waiting for transfers between devices, body(): lax.psum_scatter(sci_img - model, 'visit', scatter_dimension=1, tiled=True)  38.7 us
    all_to_all x1, starting transfers between devices, body(): lax.all_to_all(out_meta, 'sky', split_axis=0, concat_axis=0, tiled=True)  19.1 us
    all_to_all x1, starting transfers between devices, body(): lax.all_to_all(outgoing, 'sky', split_axis=0, concat_axis=0, tiled=True)  15 us
  transfers between devices with their start and end apart: 5, of which 3 were waited for; matrix products, arithmetic and copies ran while one was open for 19% of the time, Pallas kernels for 0%

commit v1 on v0

v1 whole, which is shorter than its diff:
```python
import jax
import jax.numpy as jnp
from jax import lax
from jax.experimental import pallas as pl
from jax.experimental.pallas import tpu as pltpu
from jax.sharding import PartitionSpec as P

MESH = pl.DeviceIdType.MESH
F32 = jnp.float32
TS = 128
COUNT = 56
OWNERS = 64
NB = 9
KS = 31
NX = 4
NZ = 16
STEPS = 8
MSG = 2 * TS + 8
EXT = 288


def tables_kernel(owner, cell, weight, coef, index, meta, filled):
    meta[...] = jnp.zeros(meta.shape, F32)

    @pl.loop(0, OWNERS)
    def _(o):
        filled[o] = 0
        index[2 * o] = -1
        index[2 * o + 1] = -1

    @pl.loop(0, COUNT)
    def _(t):
        o = owner[t, 0]
        k = filled[o]
        filled[o] = k + 1
        index[2 * o + k] = t
        meta[o, pl.ds(k, 1), 0 : 3 * NB] = coef[pl.ds(t, 1), :] * weight[t]
        meta[o, pl.ds(2 + k, 1), :] = jnp.full((1, TS), cell[t].astype(F32))


def place(x, y, z, c):
    return (lax.rem(y, NX) * 2 + c, lax.rem(x, NX) * NZ + lax.rem(z, NZ))


def main_kernel(
    index,
    shift,
    taps,
    weight,
    meta,
    b_rows,
    b_cols,
    raw,
    template,
    out,
    rawpad,
    snd,
    rcv,
    ysnd,
    yrcv,
    zrcv,
    fin0,
    fin1,
    halo,
    ext,
    shifted,
    middle,
    conv,
    raw_sem,
    ext_sem,
    halo_ss,
    halo_rs,
    x_ss,
    x_rs,
    y_ss,
    y_rs,
    z_ss,
    z_rs,
    f_ss,
    f_rs,
):
    visit = lax.axis_index("visit")
    sky = lax.axis_index("sky")
    y, c = visit // 2, visit % 2
    x, z = sky // NZ, sky % NZ
    pos = jnp.where(c == 0, y, x)

    def along(step):
        return place(
            jnp.where(c == 0, x, x + step), jnp.where(c == 0, y + step, y), z, c
        )

    def remote(src, dst, ss, rs, to):
        return pltpu.make_async_remote_copy(
            src_ref=src, dst_ref=dst, send_sem=ss, recv_sem=rs, device_id=to, device_id_type=MESH
        )

    raw_copy = pltpu.make_async_copy(raw, rawpad.at[:, pl.ds(8, TS), :], raw_sem)
    raw_copy.start()

    def ext_copy(k):
        block = lax.rem(visit + 7 + k, 8)
        return pltpu.make_async_copy(
            template.at[:, pl.ds(pl.multiple_of(block * TS, TS), TS)],
            ext.at[pl.ds(16, 256), pl.ds(k * TS, TS)],
            ext_sem.at[k],
        )

    for k in range(3):
        ext_copy(k).start()

    barrier = pltpu.get_barrier_semaphore()
    up, down = lax.rem(sky + 1, OWNERS), lax.rem(sky + OWNERS - 1, OWNERS)
    greeted = [(visit, up), (visit, down), place(x, y, z + 1, c), place(x, y, z + NZ - 1, c), place(x, y, z, 1 - c)]
    for a in range(1, NX):
        for d in range(2):
            greeted += [place(x + a, y, z, d), place(x, y + a, z, d)]
    for to in greeted:
        pl.semaphore_signal(barrier, inc=1, device_id=to, device_id_type=MESH)

    @pl.when(x != y)
    def _():
        for d in range(2):
            pl.semaphore_signal(barrier, inc=1, device_id=place(y, x, z, d), device_id_type=MESH)

    blank = jnp.zeros((COUNT, 8, TS), F32)
    rawpad[:, 0:8, :] = blank
    rawpad[:, TS + 8 : TS + 16, :] = blank

    pl.semaphore_wait(barrier, len(greeted) + jnp.where(x != y, 2, 0))

    halo_up = remote(template.at[pl.ds(240, 16), :], halo.at[0], halo_ss.at[0], halo_rs.at[0], (visit, up))
    halo_down = remote(template.at[pl.ds(0, 16), :], halo.at[1], halo_ss.at[1], halo_rs.at[1], (visit, down))
    halo_up.start()
    halo_down.start()
    raw_copy.wait()

    lane = lax.broadcasted_iota(jnp.int32, (1, TS), 1)

    def warp(slot):
        found = index[slot]
        t = jnp.maximum(found, 0)
        w = jnp.where(found >= 0, weight[t], 0.0)
        rows = None
        for a in range(4):
            part = rawpad[t, pl.ds(shift[t, 0] + (7 + a), TS), :] * (taps[t, 0, a] * w)
            rows = part if rows is None else rows + part
        total = None
        for a in range(4):
            d = shift[t, 1] + (a - 1)
            factor = jnp.where(jnp.logical_and(lane + d >= 0, lane + d < TS), taps[t, 1, a], 0.0)
            part = pltpu.roll(rows, lax.rem(TS - d, TS), 1) * factor
            total = part if total is None else total + part
        return total

    def x_target(m):
        a, d = m // 2, m % 2
        return place(jnp.where(d == 0, x + a, x), jnp.where(d == 0, y, y + a), z, d)

    def x_copy(j, m):
        slot = m // 2 * 2 + c
        return remote(snd.at[j, m], rcv.at[j, slot], x_ss.at[j, m], x_rs.at[j, slot], x_target(m))

    def own_copy(j):
        return pltpu.make_async_copy(snd.at[j, c], rcv.at[j, c], x_rs.at[j, c])

    def send_tiles(j):
        @pl.loop(0, 8)
        def _(m):
            a, d = m // 2, m % 2
            owner_x = lax.rem(jnp.where(d == 0, x, y) + a, NX)
            owner_z = lax.rem(jnp.where(d == 0, z + 8 - j, z + 9 + j), NZ)
            owner = owner_x * NZ + owner_z
            for k in range(2):
                snd[j, m, k * TS : (k + 1) * TS, :] = warp(2 * owner + k)
            snd[j, m, 2 * TS : MSG, :] = meta[owner]

            @pl.when(m == c)
            def _():
                own_copy(j).start()

            @pl.when(m != c)
            def _():
                x_copy(j, m).start()

    def wait_tiles(j):
        @pl.loop(0, 8)
        def _(m):
            @pl.when(m == c)
            def _():
                own_copy(j).wait()

            @pl.when(m != c)
            def _():
                remote(snd.at[j, m], rcv.at[j, m], x_ss.at[j, m], x_rs.at[j, m], x_target(m)).wait_recv()

    sub = lax.broadcasted_iota(jnp.int32, (8, TS), 0)

    def gather_cells(j, h):
        for e in range(2):
            group = lax.rem(pos + (3 - h if e == 0 else 1 + h), NX)
            coefs = []
            for r in range(2):
                cell = (r * 8 + group * 2 + e).astype(F32)
                pixels, row = None, None
                for m in range(8):
                    for k in range(2):
                        named = rcv[j, m, 2 * TS + 2 + k : 2 * TS + 3 + k, :]
                        mask = jnp.where(named == cell, 1.0, 0.0)
                        part = rcv[j, m, k * TS : (k + 1) * TS, :] * mask
                        pixels = part if pixels is None else pixels + part
                        part = rcv[j, m, 2 * TS + k : 2 * TS + 1 + k, :] * mask
                        row = part if row is None else row + part
                ysnd[j, h, e, r * TS : (r + 1) * TS, :] = pixels
                coefs.append(row)
            ysnd[j, h, e, 2 * TS : MSG, :] = jnp.where(sub == 0, coefs[0], jnp.where(sub == 1, coefs[1], 0.0))

    def y_copy(j, h, e):
        return remote(
            ysnd.at[j, h, e], yrcv.at[j, h, e], y_ss.at[j, h, e], y_rs.at[j, h, e], along(1 if e == 0 else NX - 1)
        )

    def y_send(j, h):
        for e in range(2):
            y_copy(j, h, e).start()

    def y_take(j, h):
        for e in range(2):
            y_copy(j, h - 1, e).wait_recv()
            ysnd[j, h, e] = ysnd[j, h, e] + yrcv[j, h - 1, e]

    def z_copy(j):
        to = place(x, y, jnp.where(c == 0, z + 1, z + NZ - 1), c)
        return remote(ysnd.at[j, 3], zrcv.at[j], z_ss.at[j], z_rs.at[j], to)

    def finish(j):
        y_take(j, 3)

        @pl.when(j >= 1)
        def _():
            z_copy(j - 1).wait_recv()
            ysnd[j, 3] = ysnd[j, 3] + zrcv[j - 1]

        @pl.when(jnp.logical_or(c == 0, j < STEPS - 1))
        def _():
            z_copy(j).start()

    send_tiles(0)
    send_tiles(1)

    halo_up.wait_recv()
    halo_down.wait_recv()
    for k in range(3):
        ext_copy(k).wait()
    keep_up = jnp.where(sky > 0, 1.0, 0.0)
    keep_down = jnp.where(sky < OWNERS - 1, 1.0, 0.0)
    for k in range(3):
        block = pl.multiple_of(lax.rem(visit + 7 + k, 8) * TS, TS)
        cols = slice(k * TS, (k + 1) * TS)
        ext[0:16, cols] = halo[0, :, pl.ds(block, TS)] * keep_up
        ext[272:EXT, cols] = halo[1, :, pl.ds(block, TS)] * keep_down
    ext[:, 0:TS] = ext[:, 0:TS] * jnp.where(visit > 0, 1.0, 0.0)
    ext[:, 2 * TS :] = ext[:, 2 * TS :] * jnp.where(visit < 7, 1.0, 0.0)
    for v in range(KS):
        shifted[v] = ext[:, TS - 15 + v : 2 * TS - 15 + v]

    @pl.loop(0, NB)
    def _(b):
        total = shifted[0] * b_cols[b, 0]
        for v in range(1, KS):
            total = total + shifted[v] * b_cols[b, v]
        middle[...] = total
        total = middle[1:257, :] * b_rows[b, 0]
        for u in range(1, KS):
            total = total + middle[u + 1 : u + 257, :] * b_rows[b, u]
        conv[b] = total

    @pl.loop(0, STEPS)
    def _(j):
        wait_tiles(j)
        gather_cells(j, 0)
        y_send(j, 0)

        @pl.loop(1, 4)
        def _(h):
            gather_cells(j, h)

        @pl.when(j + 2 < STEPS)
        def _():
            send_tiles(j + 2)

        @pl.when(j >= 1)
        def _():
            finish(j - 1)

        for h in range(1, 3):
            y_take(j, h)
            y_send(j, h)

    last = STEPS - 1
    finish(last)

    to_sibling = remote(zrcv.at[last, 1], fin0, f_ss.at[0], f_rs.at[0], place(x, y, z, 1))
    to_even = remote(ysnd.at[last, 3, 0], fin1, f_ss.at[1], f_rs.at[1], place(y, x, z, 0))
    to_odd = remote(ysnd.at[last, 3, 1], fin1, f_ss.at[2], f_rs.at[1], place(y, x, z, 1))
    stay_odd = pltpu.make_async_copy(ysnd.at[last, 3, 1], fin1, f_rs.at[1])

    @pl.when(c == 0)
    def _():
        z_copy(last).wait_recv()
        to_sibling.start()
        fin0[...] = zrcv[last, 0]

    @pl.when(c == 1)
    def _():
        to_even.start()

        @pl.when(x != y)
        def _():
            to_odd.start()

        @pl.when(x == y)
        def _():
            stay_odd.start()

        to_sibling.wait_recv()

    @pl.when(jnp.logical_and(c == 1, x == y))
    def _():
        stay_odd.wait()

    @pl.when(jnp.logical_not(jnp.logical_and(c == 1, x == y)))
    def _():
        to_odd.wait_recv()

    xs = (2.0 * lane.astype(F32) + 1.0) / TS - 1.0
    ys = (2.0 * lax.broadcasted_iota(jnp.int32, (TS, 1), 0).astype(F32) + 1.0) / TS - 1.0
    ys = jnp.broadcast_to(ys, (TS, TS))
    for r in range(2):
        rows = slice(r * TS, (r + 1) * TS)
        coef = fin0[2 * TS + r : 2 * TS + r + 1, :] + fin1[2 * TS + r : 2 * TS + r + 1, :]
        total = fin0[rows, :] + fin1[rows, :]
        for b in range(NB):
            flat = coef[:, 3 * b : 3 * b + 1] + coef[:, 3 * b + 1 : 3 * b + 2] * xs
            field = flat + coef[:, 3 * b + 2 : 3 * b + 3] * ys
            total = total - conv[b, rows, :] * field
        out[rows, :] = total

    halo_up.wait_send()
    halo_down.wait_send()

    @pl.loop(0, STEPS)
    def _(j):
        @pl.loop(0, 8)
        def _(m):
            @pl.when(m != c)
            def _():
                x_copy(j, m).wait_send()

        for h in range(3):
            for e in range(2):
                y_copy(j, h, e).wait_send()

        @pl.when(jnp.logical_or(c == 0, j < STEPS - 1))
        def _():
            z_copy(j).wait_send()

    @pl.when(c == 0)
    def _():
        to_sibling.wait_send()

    @pl.when(c == 1)
    def _():
        to_even.wait_send()

        @pl.when(x != y)
        def _():
            to_odd.wait_send()


def body(
    raw_tiles,
    warp_shift,
    warp_taps,
    match_coeffs,
    tile_weights,
    dest_owner,
    dest_cell,
    template,
    basis_rows,
    basis_cols,
):
    smem = pl.BlockSpec(memory_space=pltpu.SMEM)
    vmem = pl.BlockSpec(memory_space=pltpu.VMEM)
    hbm = pl.BlockSpec(memory_space=pl.ANY)
    index, meta = pl.pallas_call(
        tables_kernel,
        out_shape=(
            jax.ShapeDtypeStruct((2 * OWNERS,), jnp.int32),
            jax.ShapeDtypeStruct((OWNERS, 8, TS), F32),
        ),
        in_specs=[smem, smem, smem, vmem],
        out_specs=(smem, vmem),
        scratch_shapes=[pltpu.SMEM((OWNERS,), jnp.int32)],
        name="tables",
    )(dest_owner, dest_cell, tile_weights, match_coeffs)
    dma = pltpu.SemaphoreType.DMA
    return pl.pallas_call(
        main_kernel,
        out_shape=jax.ShapeDtypeStruct((2 * TS, TS), F32),
        in_specs=[smem, smem, smem, smem, vmem, smem, smem, hbm, hbm],
        out_specs=vmem,
        scratch_shapes=[
            pltpu.VMEM((COUNT, TS + 16, TS), F32),
            pltpu.VMEM((STEPS, 8, MSG, TS), F32),
            pltpu.VMEM((STEPS, 8, MSG, TS), F32),
            pltpu.VMEM((STEPS, 4, 2, MSG, TS), F32),
            pltpu.VMEM((STEPS, 3, 2, MSG, TS), F32),
            pltpu.VMEM((STEPS, 2, MSG, TS), F32),
            pltpu.VMEM((MSG, TS), F32),
            pltpu.VMEM((MSG, TS), F32),
            pltpu.VMEM((2, 16, 8 * TS), F32),
            pltpu.VMEM((EXT, 3 * TS), F32),
            pltpu.VMEM((KS, EXT, TS), F32),
            pltpu.VMEM((EXT, TS), F32),
            pltpu.VMEM((NB, 2 * TS, TS), F32),
            dma,
            dma((3,)),
            dma((2,)),
            dma((2,)),
            dma((STEPS, 8)),
            dma((STEPS, 8)),
            dma((STEPS, 3, 2)),
            dma((STEPS, 3, 2)),
            dma((STEPS,)),
            dma((STEPS,)),
            dma((3,)),
            dma((2,)),
        ],
        compiler_params=pltpu.CompilerParams(
            collective_id=0, has_side_effects=True, vmem_limit_bytes=58 * 2**20
        ),
        name="exchange",
    )(index, warp_shift, warp_taps, tile_weights, meta, basis_rows, basis_cols, raw_tiles, template)


def solution(mesh):
    return jax.shard_map(
        body,
        mesh=mesh,
        in_specs=(
            P(("visit", "sky"), None, None),
            P(("visit", "sky"), None),
            P(("visit", "sky"), None, None),
            P(("visit", "sky"), None),
            P(("visit", "sky")),
            P(("visit", "sky"), None),
            P(("visit", "sky")),
            P("sky", None),
            P(),
            P(),
        ),
        out_specs=P("sky", "visit"),
        check_vma=False,
    )
```

time: 602 us -> 163 us (0.27); the launches traced: 591 us -> 162 us
  waiting for transfers between devices: 392 us -> 0 us
  Pallas kernels: 0 us -> 155 us
  matrix products: 97.3 us -> 0 us
  starting transfers between devices: 39.5 us -> 0 us
  local copies, waits for them, and re-layouts: 39.8 us -> 7.12 us
  between operations: 14.6 us -> 0.02 us
  other arithmetic: 8.17 us -> 0 us
    ppermute x2 -> x0, waiting for transfers between devices: 353 us -> none  [the longest x1 350 us: extended(): before = lax.ppermute(last, axis, up)]
    pallas_call x0 -> x2, Pallas kernels: none -> 155 us  [the longest x1 151 us: body(): pl.pallas_call(main_kernel, out_shape=jax.ShapeDtypeStruct((2 * TS, TS),...]
    dot_general x32 -> x0, matrix products: 97.3 us -> none  [the longest x8 47.9 us: model_block(): jnp.einsum('bki,bkj->bij', down, middle, precision=lax.Precision.HIGHEST)]
    reduce_scatter x1 -> x0, waiting for transfers between devices: 38.7 us -> none  [body(): lax.psum_scatter(sci_img - model, 'visit', scatter_dimension=1, tiled=True)]
    all_to_all x2 -> x0, starting transfers between devices: 34.1 us -> none  [the longest x1 19.1 us: body(): lax.all_to_all(out_meta, 'sky', split_axis=0, concat_axis=0, tiled=True)]
    dot_general x4 -> x0, local copies, waits for them, and re-layouts: 18.6 us -> none  [the longest x1 8.99 us: place_cells(): sci_cells = jnp.dot(gather_cells, incoming, precision=lax.Precision.HIGHEST)]
    reshape x4 -> x0, local copies, waits for them, and re-layouts: 15.9 us -> none  [the longest x1 10.9 us: place_cells(): incoming = incoming.reshape(-1, incoming.shape[2])]
  transfers between devices with their start and end apart: 5 -> 0, of which waited for: 3 -> 0; matrix products, arithmetic and copies ran while one was open for 19% -> 0% of each run, Pallas kernels for 0% -> 0%
where the time goes in v1:
time: 163 us; the launch traced here: 162 us
  Pallas kernels  155 us (95%)
  local copies, waits for them, and re-layouts  7.12 us (4%)
    pallas_call x1, Pallas kernels, body(): pl.pallas_call(main_kernel, out_shape=jax.ShapeDtypeStruct((2 * TS, TS),...  151 us
    unnamed x5, local copies, waits for them, and re-layouts  7.12 us

profile of v1, /device:TPU:1, one launch (start us, length us, event | category | flops | bytes accessed | tf_op | source)
XLA Modules:
  0.0 161.7 jit_solution(3635336321311621893)
XLA Ops:
  0.0 1.4 copy.13.shift
  1.4 1.4 copy.12.coef
  2.8 1.3 copy.11.owner
  4.1 1.4 copy.14.taps
  5.6 3.2 %tables.1 = (s32[128]{0:T(128)}, f32[64,8,128]{2,1,0:T(8,128)}) custom-call(s32[56,1]{1,0:T(8,128)} %copy.11.owner, s32[56]{0:T(128)} %cell.1, f32[56]{0:T(128)} %weight.3, f32[56,27]{1,0:T(8,128)} %copy.12.coef), custom_call_target="tpu_custom_call" | custom-call | tf_op jit(solution)/shard_map/tables/pallas_call | solution.py:396
  8.7 151.4 %exchange.1 = f32[256,128]{1,0:T(8,128)} custom-call(s32[128]{0:T(128)} %get-tuple-element.7.index, s32[56,2]{1,0:T(8,128)} %copy.13.shift, f32[56,2,4]{2,1,0:T(2,128)} %copy.14.taps, f32[56]{0:T(128)} %weight.3, f32[64,8,128]{2,1,0:T(8,128)} %get-tuple-element.8.meta, f32[9,31]{1,0:T(8,128)} %b_rows.1, f32[9,31]{1,0:T(8,128)} %b_cols.1, ...), custom_call_target="tpu_custom_call" | custom-call | tf_op jit(solution)/shard_map/exchange/pallas_call | solution.py:408
  160.2 1.6 copy.16

commit v2 on v1

--- a/solution.py
+++ b/solution.py
@@ -16,11 +16,15 @@
 NZ = 16
 STEPS = 8
 MSG = 2 * TS + 8
+CELL = TS + 8
 EXT = 288
 
 
-def tables_kernel(owner, cell, weight, coef, index, meta, filled):
+def tables_kernel(owner, cell, weight, coef, index, meta, filled, square, by_tile):
     meta[...] = jnp.zeros(meta.shape, F32)
+    square[...] = jnp.zeros(square.shape, F32)
+    square[0 : 3 * NB, 0:COUNT] = coef[...]
+    by_tile[...] = square[...].T
 
     @pl.loop(0, OWNERS)
     def _(o):
@@ -30,11 +34,11 @@
 
     @pl.loop(0, COUNT)
     def _(t):
-        o = owner[t, 0]
+        o = owner[0, t]
         k = filled[o]
         filled[o] = k + 1
         index[2 * o + k] = t
-        meta[o, pl.ds(k, 1), 0 : 3 * NB] = coef[pl.ds(t, 1), :] * weight[t]
+        meta[o, pl.ds(k, 1), :] = by_tile[pl.ds(t, 1), :] * weight[t]
         meta[o, pl.ds(2 + k, 1), :] = jnp.full((1, TS), cell[t].astype(F32))
 
 
@@ -59,6 +63,9 @@
     ysnd,
     yrcv,
     zrcv,
+    wrcv,
+    vsnd,
+    vrcv,
     fin0,
     fin1,
     halo,
@@ -76,6 +83,10 @@
     y_rs,
     z_ss,
     z_rs,
+    w_ss,
+    w_rs,
+    v_ss,
+    v_rs,
     f_ss,
     f_rs,
 ):
@@ -143,12 +154,12 @@
         w = jnp.where(found >= 0, weight[t], 0.0)
         rows = None
         for a in range(4):
-            part = rawpad[t, pl.ds(shift[t, 0] + (7 + a), TS), :] * (taps[t, 0, a] * w)
+            part = rawpad[t, pl.ds(shift[0, t] + (7 + a), TS), :] * (taps[0, a, t] * w)
             rows = part if rows is None else rows + part
         total = None
         for a in range(4):
-            d = shift[t, 1] + (a - 1)
-            factor = jnp.where(jnp.logical_and(lane + d >= 0, lane + d < TS), taps[t, 1, a], 0.0)
+            d = shift[1, t] + (a - 1)
+            factor = jnp.where(jnp.logical_and(lane + d >= 0, lane + d < TS), taps[1, a, t], 0.0)
             part = pltpu.roll(rows, lax.rem(TS - d, TS), 1) * factor
             total = part if total is None else total + part
         return total
@@ -164,10 +175,11 @@
     def own_copy(j):
         return pltpu.make_async_copy(snd.at[j, c], rcv.at[j, c], x_rs.at[j, c])
 
-    def send_tiles(j):
-        @pl.loop(0, 8)
-        def _(m):
-            a, d = m // 2, m % 2
+    def send_tiles(j, first=0, end=8):
+        @pl.loop(first, end)
+        def _(i):
+            a, d = jnp.where(i < 4, i // 2 * 2 + 1, 6 - i // 2 * 2), i % 2
+            m = 2 * a + d
             owner_x = lax.rem(jnp.where(d == 0, x, y) + a, NX)
             owner_z = lax.rem(jnp.where(d == 0, z + 8 - j, z + 9 + j), NZ)
             owner = owner_x * NZ + owner_z
@@ -197,10 +209,9 @@
     sub = lax.broadcasted_iota(jnp.int32, (8, TS), 0)
 
     def gather_cells(j, h):
-        for e in range(2):
-            group = lax.rem(pos + (3 - h if e == 0 else 1 + h), NX)
-            coefs = []
-            for r in range(2):
+        for r in range(2):
+            group = lax.rem(pos + (3 - h if r == 0 else 1 + h), NX)
+            for e in range(2):
                 cell = (r * 8 + group * 2 + e).astype(F32)
                 pixels, row = None, None
                 for m in range(8):
@@ -211,27 +222,26 @@
                         pixels = part if pixels is None else pixels + part
                         part = rcv[j, m, 2 * TS + k : 2 * TS + 1 + k, :] * mask
                         row = part if row is None else row + part
-                ysnd[j, h, e, r * TS : (r + 1) * TS, :] = pixels
-                coefs.append(row)
-            ysnd[j, h, e, 2 * TS : MSG, :] = jnp.where(sub == 0, coefs[0], jnp.where(sub == 1, coefs[1], 0.0))
-
-    def y_copy(j, h, e):
-        return remote(
-            ysnd.at[j, h, e], yrcv.at[j, h, e], y_ss.at[j, h, e], y_rs.at[j, h, e], along(1 if e == 0 else NX - 1)
-        )
+                ysnd[j, h, e, r, 0:TS, :] = pixels
+                ysnd[j, h, e, r, TS:CELL, :] = jnp.where(sub == 0, row, 0.0)
+
+    def y_copy(j, h, r):
+        to = along(1 if r == 0 else NX - 1)
+        return remote(ysnd.at[j, h, 0, r], yrcv.at[j, h, r], y_ss.at[j, h, r], y_rs.at[j, h, r], to)
 
     def y_send(j, h):
-        for e in range(2):
-            y_copy(j, h, e).start()
+        for r in range(2):
+            y_copy(j, h, r).start()
 
     def y_take(j, h):
-        for e in range(2):
-            y_copy(j, h - 1, e).wait_recv()
-            ysnd[j, h, e] = ysnd[j, h, e] + yrcv[j, h - 1, e]
+        for r in range(2):
+            y_copy(j, h - 1, r).wait_recv()
+            ysnd[j, h, 0, r] = ysnd[j, h, 0, r] + yrcv[j, h - 1, r]
+
+    onward = place(x, y, jnp.where(c == 0, z + 1, z + NZ - 1), c)
 
     def z_copy(j):
-        to = place(x, y, jnp.where(c == 0, z + 1, z + NZ - 1), c)
-        return remote(ysnd.at[j, 3], zrcv.at[j], z_ss.at[j], z_rs.at[j], to)
+        return remote(ysnd.at[j, 3, 0], zrcv.at[j], z_ss.at[j], z_rs.at[j], onward)
 
     def finish(j):
         y_take(j, 3)
@@ -239,11 +249,47 @@
         @pl.when(j >= 1)
         def _():
             z_copy(j - 1).wait_recv()
-            ysnd[j, 3] = ysnd[j, 3] + zrcv[j - 1]
+            ysnd[j, 3, 0] = ysnd[j, 3, 0] + zrcv[j - 1]
 
         @pl.when(jnp.logical_or(c == 0, j < STEPS - 1))
         def _():
             z_copy(j).start()
+
+    def w_copy(j, h):
+        return remote(ysnd.at[j, h, 1], wrcv.at[j, h], w_ss.at[j, h], w_rs.at[j, h], onward)
+
+    def carry(j):
+        @pl.loop(0, 4)
+        def _(h):
+            @pl.when(j >= 1)
+            def _():
+                w_copy(j - 1, h).wait_recv()
+                ysnd[j, h, 1] = ysnd[j, h, 1] + wrcv[j - 1, h]
+
+            @pl.when(jnp.logical_or(c == 0, j < STEPS - 1))
+            def _():
+                w_copy(j, h).start()
+
+    def v_copy(h, r):
+        to = along(1 if r == 0 else NX - 1)
+        return remote(vsnd.at[h, r], vrcv.at[h, r], v_ss.at[h, r], v_rs.at[h, r], to)
+
+    def v_step(h):
+        @pl.when(c == 0)
+        def _():
+            w_copy(STEPS - 1, h).wait_recv()
+            vsnd[h] = wrcv[STEPS - 1, h]
+
+        @pl.when(c == 1)
+        def _():
+            vsnd[h] = ysnd[STEPS - 1, h, 1]
+
+        for r in range(2):
+            if h >= 1:
+                v_copy(h - 1, r).wait_recv()
+                vsnd[h, r] = vsnd[h, r] + vrcv[h - 1, r]
+            if h < 3:
+                v_copy(h, r).start()
 
     send_tiles(0)
     send_tiles(1)
@@ -264,8 +310,7 @@
     for v in range(KS):
         shifted[v] = ext[:, TS - 15 + v : 2 * TS - 15 + v]
 
-    @pl.loop(0, NB)
-    def _(b):
+    def convolve(b):
         total = shifted[0] * b_cols[b, 0]
         for v in range(1, KS):
             total = total + shifted[v] * b_cols[b, v]
@@ -275,46 +320,69 @@
             total = total + middle[u + 1 : u + 257, :] * b_rows[b, u]
         conv[b] = total
 
+    convolve(STEPS)
+
     @pl.loop(0, STEPS)
     def _(j):
         wait_tiles(j)
         gather_cells(j, 0)
         y_send(j, 0)
+        for h in range(1, 3):
+
+            @pl.when(j >= h)
+            def _():
+                y_take(j - h, h)
+                y_send(j - h, h)
+
+        @pl.when(j >= 3)
+        def _():
+            finish(j - 3)
 
         @pl.loop(1, 4)
         def _(h):
             gather_cells(j, h)
 
+        carry(j)
+
         @pl.when(j + 2 < STEPS)
         def _():
             send_tiles(j + 2)
 
-        @pl.when(j >= 1)
-        def _():
-            finish(j - 1)
-
-        for h in range(1, 3):
-            y_take(j, h)
-            y_send(j, h)
+        convolve(j)
 
     last = STEPS - 1
+    to_sibling = remote(vsnd.at[3], fin0, f_ss.at[0], f_rs.at[0], place(x, y, z, 1))
+    to_even = remote(ysnd.at[last, 3, 0], fin1, f_ss.at[1], f_rs.at[1], place(y, x, z, 0))
+    to_odd = remote(vsnd.at[3], fin1, f_ss.at[2], f_rs.at[1], place(y, x, z, 1))
+    stay_odd = pltpu.make_async_copy(vsnd.at[3], fin1, f_rs.at[1])
+
+    y_take(last, 1)
+    y_send(last, 1)
+    y_take(last - 1, 2)
+    y_send(last - 1, 2)
+    finish(last - 2)
+    v_step(0)
+    y_take(last, 2)
+    y_send(last, 2)
+    v_step(1)
+    finish(last - 1)
+    v_step(2)
     finish(last)
 
-    to_sibling = remote(zrcv.at[last, 1], fin0, f_ss.at[0], f_rs.at[0], place(x, y, z, 1))
-    to_even = remote(ysnd.at[last, 3, 0], fin1, f_ss.at[1], f_rs.at[1], place(y, x, z, 0))
-    to_odd = remote(ysnd.at[last, 3, 1], fin1, f_ss.at[2], f_rs.at[1], place(y, x, z, 1))
-    stay_odd = pltpu.make_async_copy(ysnd.at[last, 3, 1], fin1, f_rs.at[1])
+    @pl.when(c == 1)
+    def _():
+        to_even.start()
+
+    v_step(3)
 
     @pl.when(c == 0)
     def _():
+        to_sibling.start()
         z_copy(last).wait_recv()
-        to_sibling.start()
-        fin0[...] = zrcv[last, 0]
+        fin0[...] = zrcv[last]
 
     @pl.when(c == 1)
     def _():
-        to_even.start()
-
         @pl.when(x != y)
         def _():
             to_odd.start()
@@ -338,8 +406,8 @@
     ys = jnp.broadcast_to(ys, (TS, TS))
     for r in range(2):
         rows = slice(r * TS, (r + 1) * TS)
-        coef = fin0[2 * TS + r : 2 * TS + r + 1, :] + fin1[2 * TS + r : 2 * TS + r + 1, :]
-        total = fin0[rows, :] + fin1[rows, :]
+        coef = fin0[r, TS : TS + 1, :] + fin1[r, TS : TS + 1, :]
+        total = fin0[r, 0:TS, :] + fin1[r, 0:TS, :]
         for b in range(NB):
             flat = coef[:, 3 * b : 3 * b + 1] + coef[:, 3 * b + 1 : 3 * b + 2] * xs
             field = flat + coef[:, 3 * b + 2 : 3 * b + 3] * ys
@@ -358,12 +426,18 @@
                 x_copy(j, m).wait_send()
 
         for h in range(3):
-            for e in range(2):
-                y_copy(j, h, e).wait_send()
+            for r in range(2):
+                y_copy(j, h, r).wait_send()
 
         @pl.when(jnp.logical_or(c == 0, j < STEPS - 1))
         def _():
             z_copy(j).wait_send()
+            for h in range(4):
+                w_copy(j, h).wait_send()
+
+    for h in range(3):
+        for r in range(2):
+            v_copy(h, r).wait_send()
 
     @pl.when(c == 0)
     def _():
@@ -401,9 +475,13 @@
         ),
         in_specs=[smem, smem, smem, vmem],
         out_specs=(smem, vmem),
-        scratch_shapes=[pltpu.SMEM((OWNERS,), jnp.int32)],
+        scratch_shapes=[
+            pltpu.SMEM((OWNERS,), jnp.int32),
+            pltpu.VMEM((TS, TS), F32),
+            pltpu.VMEM((TS, TS), F32),
+        ],
         name="tables",
-    )(dest_owner, dest_cell, tile_weights, match_coeffs)
+    )(dest_owner.T, dest_cell, tile_weights, match_coeffs.T)
     dma = pltpu.SemaphoreType.DMA
     return pl.pallas_call(
         main_kernel,
@@ -414,11 +492,14 @@
             pltpu.VMEM((COUNT, TS + 16, TS), F32),
             pltpu.VMEM((STEPS, 8, MSG, TS), F32),
             pltpu.VMEM((STEPS, 8, MSG, TS), F32),
-            pltpu.VMEM((STEPS, 4, 2, MSG, TS), F32),
-            pltpu.VMEM((STEPS, 3, 2, MSG, TS), F32),
-            pltpu.VMEM((STEPS, 2, MSG, TS), F32),
-            pltpu.VMEM((MSG, TS), F32),
-            pltpu.VMEM((MSG, TS), F32),
+            pltpu.VMEM((STEPS, 4, 2, 2, CELL, TS), F32),
+            pltpu.VMEM((STEPS, 3, 2, CELL, TS), F32),
+            pltpu.VMEM((STEPS, 2, CELL, TS), F32),
+            pltpu.VMEM((STEPS, 4, 2, CELL, TS), F32),
+            pltpu.VMEM((4, 2, CELL, TS), F32),
+            pltpu.VMEM((3, 2, CELL, TS), F32),
+            pltpu.VMEM((2, CELL, TS), F32),
+            pltpu.VMEM((2, CELL, TS), F32),
             pltpu.VMEM((2, 16, 8 * TS), F32),
             pltpu.VMEM((EXT, 3 * TS), F32),
             pltpu.VMEM((KS, EXT, TS), F32),
@@ -434,6 +515,10 @@
             dma((STEPS, 3, 2)),
             dma((STEPS,)),
             dma((STEPS,)),
+            dma((STEPS, 4)),
+            dma((STEPS, 4)),
+            dma((3, 2)),
+            dma((3, 2)),
             dma((3,)),
             dma((2,)),
         ],
@@ -441,7 +526,17 @@
             collective_id=0, has_side_effects=True, vmem_limit_bytes=58 * 2**20
         ),
         name="exchange",
-    )(index, warp_shift, warp_taps, tile_weights, meta, basis_rows, basis_cols, raw_tiles, template)
+    )(
+        index,
+        warp_shift.T,
+        jnp.transpose(warp_taps, (1, 2, 0)),
+        tile_weights,
+        meta,
+        basis_rows,
+        basis_cols,
+        raw_tiles,
+        template,
+    )
 
 
 def solution(mesh):

time: 163 us -> 112 us (0.69)
  Pallas kernels: 155 us -> 110 us
  local copies, waits for them, and re-layouts: 7.12 us -> 1.57 us
    pallas_call x1, Pallas kernels: 151 us -> 107 us  [body(): pl.pallas_call(main_kernel, out_shape=jax.ShapeDtypeStruct((2 * TS, TS),...]
    unnamed x5 -> x1, local copies, waits for them, and re-layouts: 7.12 us -> 1.57 us
where the time goes in v2:
time: 112 us
  Pallas kernels  110 us (98%)
  local copies, waits for them, and re-layouts  1.57 us (1%)
    pallas_call x1, Pallas kernels, body(): pl.pallas_call(main_kernel, out_shape=jax.ShapeDtypeStruct((2 * TS, TS),...  107 us
    pallas_call x1, Pallas kernels, body(): pl.pallas_call(tables_kernel, out_shape=(jax.ShapeDtypeStruct((2 * OWNERS...  2.8 us

profile of v2, /device:TPU:1, one launch (start us, length us, event | category | flops | bytes accessed | tf_op | source)
XLA Modules:
  0.0 111.8 jit_solution(6187114890911292987)
XLA Ops:
  0.0 2.8 %tables.1 = (s32[128]{0:T(128)}, f32[64,8,128]{2,1,0:T(8,128)}) custom-call(s32[1,56]{1,0:T(1,128)} %bitcast.7, s32[56]{0:T(128)} %cell.1, f32[56]{0:T(128)} %weight.3, f32[27,56]{1,0:T(8,128)} %bitcast.4), custom_call_target="tpu_custom_call" | custom-call | tf_op jit(solution)/shard_map/tables/pallas_call | solution.py:470
  2.8 107.4 %exchange.1 = f32[256,128]{1,0:T(8,128)} custom-call(s32[128]{0:T(128)} %get-tuple-element.7.index, s32[2,56]{1,0:T(2,128)} %bitcast.6, f32[2,4,56]{2,1,0:T(4,128)} %bitcast.5, f32[56]{0:T(128)} %weight.3, f32[64,8,128]{2,1,0:T(8,128)} %get-tuple-element.8.meta, f32[9,31]{1,0:T(8,128)} %b_rows.1, f32[9,31]{1,0:T(8,128)} %b_cols.1, f32[56,128,128]{2,1,0:T(8,128)} %raw.1, ...), custom_call_target="tpu_custom_call" | custom-call | tf_op jit(solution)/shard_map/exchange/pallas_call | solution.py:486
  110.2 1.6 %copy.12 = f32[256,128]{1,0:T(8,128)} copy(f32[256,128]{1,0:T(8,128)} %exchange.1) | data formatting | bytes 262144

commit v3 on v2

--- a/solution.py
+++ b/solution.py
@@ -20,17 +20,26 @@
 EXT = 288
 
 
-def tables_kernel(owner, cell, weight, coef, index, meta, filled, square, by_tile):
+def tables_kernel(
+    owner_hbm, cell_hbm, weight_hbm, coef_hbm, index, meta, owner, cell, weight, coef, filled, square, by_tile, in_sem
+):
+    small = [(owner_hbm, owner), (cell_hbm, cell), (weight_hbm, weight), (coef_hbm, coef)]
+    small = [pltpu.make_async_copy(src, dst, in_sem.at[i]) for i, (src, dst) in enumerate(small)]
+    for copy in small:
+        copy.start()
     meta[...] = jnp.zeros(meta.shape, F32)
     square[...] = jnp.zeros(square.shape, F32)
-    square[0 : 3 * NB, 0:COUNT] = coef[...]
-    by_tile[...] = square[...].T
 
     @pl.loop(0, OWNERS)
     def _(o):
         filled[o] = 0
         index[2 * o] = -1
         index[2 * o + 1] = -1
+
+    for copy in small:
+        copy.wait()
+    square[0 : 3 * NB, 0:COUNT] = coef[...]
+    by_tile[...] = square[...].T
 
     @pl.loop(0, COUNT)
     def _(t):
@@ -47,6 +56,16 @@
 
 
 def main_kernel(
+    index_hbm,
+    shift_hbm,
+    taps_hbm,
+    weight_hbm,
+    meta_hbm,
+    b_rows_hbm,
+    b_cols_hbm,
+    raw,
+    template,
+    out,
     index,
     shift,
     taps,
@@ -54,9 +73,6 @@
     meta,
     b_rows,
     b_cols,
-    raw,
-    template,
-    out,
     rawpad,
     snd,
     rcv,
@@ -64,7 +80,6 @@
     yrcv,
     zrcv,
     wrcv,
-    vsnd,
     vrcv,
     fin0,
     fin1,
@@ -73,6 +88,7 @@
     shifted,
     middle,
     conv,
+    in_sem,
     raw_sem,
     ext_sem,
     halo_ss,
@@ -106,6 +122,11 @@
             src_ref=src, dst_ref=dst, send_sem=ss, recv_sem=rs, device_id=to, device_id_type=MESH
         )
 
+    small = [(index_hbm, index), (shift_hbm, shift), (taps_hbm, taps), (weight_hbm, weight), (meta_hbm, meta)]
+    small += [(b_rows_hbm, b_rows), (b_cols_hbm, b_cols)]
+    small = [pltpu.make_async_copy(src, dst, in_sem.at[i]) for i, (src, dst) in enumerate(small)]
+    for copy in small:
+        copy.start()
     raw_copy = pltpu.make_async_copy(raw, rawpad.at[:, pl.ds(8, TS), :], raw_sem)
     raw_copy.start()
 
@@ -122,7 +143,9 @@
 
     barrier = pltpu.get_barrier_semaphore()
     up, down = lax.rem(sky + 1, OWNERS), lax.rem(sky + OWNERS - 1, OWNERS)
-    greeted = [(visit, up), (visit, down), place(x, y, z + 1, c), place(x, y, z + NZ - 1, c), place(x, y, z, 1 - c)]
+    greeted = [(visit, up), (visit, down), place(x, y, z, 1 - c)]
+    for d in range(2):
+        greeted += [place(x, y, z + 1, d), place(x, y, z + NZ - 1, d)]
     for a in range(1, NX):
         for d in range(2):
             greeted += [place(x + a, y, z, d), place(x, y + a, z, d)]
@@ -145,6 +168,8 @@
     halo_up.start()
     halo_down.start()
     raw_copy.wait()
+    for copy in small:
+        copy.wait()
 
     lane = lax.broadcasted_iota(jnp.int32, (1, TS), 1)
 
@@ -266,30 +291,42 @@
                 w_copy(j - 1, h).wait_recv()
                 ysnd[j, h, 1] = ysnd[j, h, 1] + wrcv[j - 1, h]
 
-            @pl.when(jnp.logical_or(c == 0, j < STEPS - 1))
+            @pl.when(j < STEPS - 1)
             def _():
                 w_copy(j, h).start()
 
     def v_copy(h, r):
         to = along(1 if r == 0 else NX - 1)
-        return remote(vsnd.at[h, r], vrcv.at[h, r], v_ss.at[h, r], v_rs.at[h, r], to)
+        return remote(ysnd.at[last, h, 1, r], vrcv.at[h, r], v_ss.at[h, r], v_rs.at[h, r], to)
 
     def v_step(h):
-        @pl.when(c == 0)
-        def _():
-            w_copy(STEPS - 1, h).wait_recv()
-            vsnd[h] = wrcv[STEPS - 1, h]
-
-        @pl.when(c == 1)
-        def _():
-            vsnd[h] = ysnd[STEPS - 1, h, 1]
-
         for r in range(2):
             if h >= 1:
                 v_copy(h - 1, r).wait_recv()
-                vsnd[h, r] = vsnd[h, r] + vrcv[h - 1, r]
+                ysnd[last, h, 1, r] = ysnd[last, h, 1, r] + vrcv[h - 1, r]
             if h < 3:
                 v_copy(h, r).start()
+
+    last = STEPS - 1
+    def sent(j):
+        @pl.loop(0, 8)
+        def _(m):
+            @pl.when(m != c)
+            def _():
+                x_copy(j, m).wait_send()
+
+        for h in range(3):
+            for r in range(2):
+                y_copy(j, h, r).wait_send()
+
+        @pl.when(jnp.logical_or(c == 0, j < STEPS - 1))
+        def _():
+            z_copy(j).wait_send()
+
+        @pl.when(j < STEPS - 1)
+        def _():
+            for h in range(4):
+                w_copy(j, h).wait_send()
 
     send_tiles(0)
     send_tiles(1)
@@ -320,6 +357,7 @@
             total = total + middle[u + 1 : u + 257, :] * b_rows[b, u]
         conv[b] = total
 
+    convolve(STEPS - 1)
     convolve(STEPS)
 
     @pl.loop(0, STEPS)
@@ -348,25 +386,30 @@
         def _():
             send_tiles(j + 2)
 
-        convolve(j)
-
-    last = STEPS - 1
-    to_sibling = remote(vsnd.at[3], fin0, f_ss.at[0], f_rs.at[0], place(x, y, z, 1))
+        @pl.when(j >= 4)
+        def _():
+            sent(j - 4)
+
+        @pl.when(j < STEPS - 1)
+        def _():
+            convolve(j)
+
+    to_next = remote(ysnd.at[last, 3, 1], fin0, f_ss.at[0], f_rs.at[0], place(x, y, z + 1, 1))
     to_even = remote(ysnd.at[last, 3, 0], fin1, f_ss.at[1], f_rs.at[1], place(y, x, z, 0))
-    to_odd = remote(vsnd.at[3], fin1, f_ss.at[2], f_rs.at[1], place(y, x, z, 1))
-    stay_odd = pltpu.make_async_copy(vsnd.at[3], fin1, f_rs.at[1])
-
+    to_odd = remote(ysnd.at[last, 3, 1], fin1, f_ss.at[2], f_rs.at[1], place(y, x, z, 1))
+    stay_odd = pltpu.make_async_copy(ysnd.at[last, 3, 1], fin1, f_rs.at[1])
+
+    v_step(0)
     y_take(last, 1)
     y_send(last, 1)
     y_take(last - 1, 2)
     y_send(last - 1, 2)
     finish(last - 2)
-    v_step(0)
+    v_step(1)
     y_take(last, 2)
     y_send(last, 2)
-    v_step(1)
+    v_step(2)
     finish(last - 1)
-    v_step(2)
     finish(last)
 
     @pl.when(c == 1)
@@ -377,7 +420,7 @@
 
     @pl.when(c == 0)
     def _():
-        to_sibling.start()
+        to_next.start()
         z_copy(last).wait_recv()
         fin0[...] = zrcv[last]
 
@@ -391,7 +434,7 @@
         def _():
             stay_odd.start()
 
-        to_sibling.wait_recv()
+        to_next.wait_recv()
 
     @pl.when(jnp.logical_and(c == 1, x == y))
     def _():
@@ -417,23 +460,9 @@
     halo_up.wait_send()
     halo_down.wait_send()
 
-    @pl.loop(0, STEPS)
+    @pl.loop(STEPS - 4, STEPS)
     def _(j):
-        @pl.loop(0, 8)
-        def _(m):
-            @pl.when(m != c)
-            def _():
-                x_copy(j, m).wait_send()
-
-        for h in range(3):
-            for r in range(2):
-                y_copy(j, h, r).wait_send()
-
-        @pl.when(jnp.logical_or(c == 0, j < STEPS - 1))
-        def _():
-            z_copy(j).wait_send()
-            for h in range(4):
-                w_copy(j, h).wait_send()
+        sent(j)
 
     for h in range(3):
         for r in range(2):
@@ -441,7 +470,7 @@
 
     @pl.when(c == 0)
     def _():
-        to_sibling.wait_send()
+        to_next.wait_send()
 
     @pl.when(c == 1)
     def _():
@@ -473,12 +502,17 @@
             jax.ShapeDtypeStruct((2 * OWNERS,), jnp.int32),
             jax.ShapeDtypeStruct((OWNERS, 8, TS), F32),
         ),
-        in_specs=[smem, smem, smem, vmem],
+        in_specs=[hbm] * 4,
         out_specs=(smem, vmem),
         scratch_shapes=[
+            pltpu.SMEM((1, COUNT), jnp.int32),
+            pltpu.SMEM((COUNT,), jnp.int32),
+            pltpu.SMEM((COUNT,), F32),
+            pltpu.VMEM((3 * NB, COUNT), F32),
             pltpu.SMEM((OWNERS,), jnp.int32),
             pltpu.VMEM((TS, TS), F32),
             pltpu.VMEM((TS, TS), F32),
+            pltpu.SemaphoreType.DMA((4,)),
         ],
         name="tables",
     )(dest_owner.T, dest_cell, tile_weights, match_coeffs.T)
@@ -486,9 +520,16 @@
     return pl.pallas_call(
         main_kernel,
         out_shape=jax.ShapeDtypeStruct((2 * TS, TS), F32),
-        in_specs=[smem, smem, smem, smem, vmem, smem, smem, hbm, hbm],
+        in_specs=[hbm] * 9,
         out_specs=vmem,
         scratch_shapes=[
+            pltpu.SMEM((2 * OWNERS,), jnp.int32),
+            pltpu.SMEM((2, COUNT), jnp.int32),
+            pltpu.SMEM((2, 4, COUNT), F32),
+            pltpu.SMEM((COUNT,), F32),
+            pltpu.VMEM((OWNERS, 8, TS), F32),
+            pltpu.SMEM((NB, KS), F32),
+            pltpu.SMEM((NB, KS), F32),
             pltpu.VMEM((COUNT, TS + 16, TS), F32),
             pltpu.VMEM((STEPS, 8, MSG, TS), F32),
             pltpu.VMEM((STEPS, 8, MSG, TS), F32),
@@ -496,7 +537,6 @@
             pltpu.VMEM((STEPS, 3, 2, CELL, TS), F32),
             pltpu.VMEM((STEPS, 2, CELL, TS), F32),
             pltpu.VMEM((STEPS, 4, 2, CELL, TS), F32),
-            pltpu.VMEM((4, 2, CELL, TS), F32),
             pltpu.VMEM((3, 2, CELL, TS), F32),
             pltpu.VMEM((2, CELL, TS), F32),
             pltpu.VMEM((2, CELL, TS), F32),
@@ -505,6 +545,7 @@
             pltpu.VMEM((KS, EXT, TS), F32),
             pltpu.VMEM((EXT, TS), F32),
             pltpu.VMEM((NB, 2 * TS, TS), F32),
+            dma((7,)),
             dma,
             dma((3,)),
             dma((2,)),

time: 112 us -> 109 us (0.973)
  the two profiles are of different devices: /device:TPU:1 before, /device:TPU:73 now
where the time goes in v3:
time: 109 us
  Pallas kernels  107 us (98%)
  local copies, waits for them, and re-layouts  1.57 us (1%)
    pallas_call x1, Pallas kernels, body(): pl.pallas_call(main_kernel, out_shape=jax.ShapeDtypeStruct((2 * TS, TS),...  105 us
    pallas_call x1, Pallas kernels, body(): pl.pallas_call(tables_kernel, out_shape=(jax.ShapeDtypeStruct((2 * OWNERS...  2.3 us

profile of v3, /device:TPU:73, one launch (start us, length us, event | category | flops | bytes accessed | tf_op | source)
XLA Modules:
  0.0 109.0 jit_solution(8144243121930301464)
XLA Ops:
  0.0 2.3 %tables.1 = (s32[128]{0:T(128)}, f32[64,8,128]{2,1,0:T(8,128)}) custom-call(s32[1,56]{1,0:T(1,128)} %bitcast.7, s32[56]{0:T(128)} %cell_hbm.1, f32[56]{0:T(128)} %weight_hbm.3, f32[27,56]{1,0:T(8,128)} %bitcast.4), custom_call_target="tpu_custom_call" | custom-call | tf_op jit(solution)/shard_map/tables/pallas_call | solution.py:499
  2.3 105.1 %exchange.1 = f32[256,128]{1,0:T(8,128)} custom-call(s32[128]{0:T(128)} %get-tuple-element.7.index_hbm, s32[2,56]{1,0:T(2,128)} %bitcast.6, f32[2,4,56]{2,1,0:T(4,128)} %bitcast.5, f32[56]{0:T(128)} %weight_hbm.3, f32[64,8,128]{2,1,0:T(8,128)} %get-tuple-element.8.meta_hbm, f32[9,31]{1,0:T(8,128)} %b_rows_hbm.1, f32[9,31]{1,0:T(8,128)} %b_cols_hbm.1, ...), custom_call_target="tpu_custom_call" | custom-call | tf_op jit(solution)/shard_map/exchange/pallas_call | solution.py:520
  107.5 1.6 %copy.12 = f32[256,128]{1,0:T(8,128)} copy(f32[256,128]{1,0:T(8,128)} %exchange.1) | data formatting | bytes 262144

commit v4 on v3

--- a/solution.py
+++ b/solution.py
@@ -122,25 +122,6 @@
             src_ref=src, dst_ref=dst, send_sem=ss, recv_sem=rs, device_id=to, device_id_type=MESH
         )
 
-    small = [(index_hbm, index), (shift_hbm, shift), (taps_hbm, taps), (weight_hbm, weight), (meta_hbm, meta)]
-    small += [(b_rows_hbm, b_rows), (b_cols_hbm, b_cols)]
-    small = [pltpu.make_async_copy(src, dst, in_sem.at[i]) for i, (src, dst) in enumerate(small)]
-    for copy in small:
-        copy.start()
-    raw_copy = pltpu.make_async_copy(raw, rawpad.at[:, pl.ds(8, TS), :], raw_sem)
-    raw_copy.start()
-
-    def ext_copy(k):
-        block = lax.rem(visit + 7 + k, 8)
-        return pltpu.make_async_copy(
-            template.at[:, pl.ds(pl.multiple_of(block * TS, TS), TS)],
-            ext.at[pl.ds(16, 256), pl.ds(k * TS, TS)],
-            ext_sem.at[k],
-        )
-
-    for k in range(3):
-        ext_copy(k).start()
-
     barrier = pltpu.get_barrier_semaphore()
     up, down = lax.rem(sky + 1, OWNERS), lax.rem(sky + OWNERS - 1, OWNERS)
     greeted = [(visit, up), (visit, down), place(x, y, z, 1 - c)]
@@ -156,6 +137,25 @@
     def _():
         for d in range(2):
             pl.semaphore_signal(barrier, inc=1, device_id=place(y, x, z, d), device_id_type=MESH)
+
+    small = [(index_hbm, index), (shift_hbm, shift), (taps_hbm, taps), (weight_hbm, weight), (meta_hbm, meta)]
+    small += [(b_rows_hbm, b_rows), (b_cols_hbm, b_cols)]
+    small = [pltpu.make_async_copy(src, dst, in_sem.at[i]) for i, (src, dst) in enumerate(small)]
+    for copy in small:
+        copy.start()
+    raw_copy = pltpu.make_async_copy(raw, rawpad.at[:, pl.ds(8, TS), :], raw_sem)
+    raw_copy.start()
+
+    def ext_copy(k):
+        block = lax.rem(visit + 7 + k, 8)
+        return pltpu.make_async_copy(
+            template.at[:, pl.ds(pl.multiple_of(block * TS, TS), TS)],
+            ext.at[pl.ds(16, 256), pl.ds(k * TS, TS)],
+            ext_sem.at[k],
+        )
+
+    for k in range(3):
+        ext_copy(k).start()
 
     blank = jnp.zeros((COUNT, 8, TS), F32)
     rawpad[:, 0:8, :] = blank

time: 109 us -> 109 us (level)
  no operation moved by 1% of the time
where the time goes in v4:
time: 109 us
  Pallas kernels  108 us (99%)
  local copies, waits for them, and re-layouts  1.57 us (1%)
    pallas_call x1, Pallas kernels, body(): pl.pallas_call(main_kernel, out_shape=jax.ShapeDtypeStruct((2 * TS, TS),...  105 us
    pallas_call x1, Pallas kernels, body(): pl.pallas_call(tables_kernel, out_shape=(jax.ShapeDtypeStruct((2 * OWNERS...  2.3 us

profile of v4, /device:TPU:73, one launch (start us, length us, event | category | flops | bytes accessed | tf_op | source)
XLA Modules:
  0.0 109.2 jit_solution(16208276674883976144)
XLA Ops:
  0.0 2.3 %tables.1 = (s32[128]{0:T(128)}, f32[64,8,128]{2,1,0:T(8,128)}) custom-call(s32[1,56]{1,0:T(1,128)} %bitcast.7, s32[56]{0:T(128)} %cell_hbm.1, f32[56]{0:T(128)} %weight_hbm.3, f32[27,56]{1,0:T(8,128)} %bitcast.4), custom_call_target="tpu_custom_call" | custom-call | tf_op jit(solution)/shard_map/tables/pallas_call | solution.py:499
  2.3 105.3 %exchange.1 = f32[256,128]{1,0:T(8,128)} custom-call(s32[128]{0:T(128)} %get-tuple-element.7.index_hbm, s32[2,56]{1,0:T(2,128)} %bitcast.6, f32[2,4,56]{2,1,0:T(4,128)} %bitcast.5, f32[56]{0:T(128)} %weight_hbm.3, f32[64,8,128]{2,1,0:T(8,128)} %get-tuple-element.8.meta_hbm, f32[9,31]{1,0:T(8,128)} %b_rows_hbm.1, f32[9,31]{1,0:T(8,128)} %b_cols_hbm.1, ...), custom_call_target="tpu_custom_call" | custom-call | tf_op jit(solution)/shard_map/exchange/pallas_call | solution.py:520
  107.6 1.6 %copy.12 = f32[256,128]{1,0:T(8,128)} copy(f32[256,128]{1,0:T(8,128)} %exchange.1) | data formatting | bytes 262144
